TPU v7x, 128 devices: a whole 4x4x4 slice. The times are simulated.
128 devices in a mesh: grp: 8 (over z, x_hi), tp: 16 (over y, x_lo, core).
Axes of the slice: x: 4 (x_hi: 2, x_lo: 2; x = x_hi * 2 + x_lo), y: 4, z: 4, core: 2. Of those that a mesh axis runs over, the one named last changes fastest.
Arguments:
- tokens_in: bfloat16 [2048, 4096], P('tp', 'grp'), may hold values from -6 to 6
- queries: bfloat16 [2048, 4096], P('tp', 'grp'), may hold values from -13 to 13
- keys_all: bfloat16 [2048, 4096], P('tp', 'grp'), may hold values from -4 to 4
- values_all: bfloat16 [2048, 4096], P('tp', 'grp'), may hold values from -24 to 24
- out_proj: bfloat16 [4096, 4096], P('grp'), may hold values from -0.375 to 0.375
- domain_ids: int32 [2048, 1], P('tp'), may hold values from 0 to 7; in each aligned block of 128 rows (0 to 127, 128 to 255, ...) at most 32 rows name the same one
- expert_domain: int32 [8], replicated, may hold values from 0 to 7, each once
- gate_proj: bfloat16 [8, 4096, 14336], P('grp', None, 'tp'), may hold values from -0.09375 to 0.09375
- up_proj: bfloat16 [8, 4096, 14336], P('grp', None, 'tp'), may hold values from -0.09375 to 0.09375
- down_proj: bfloat16 [8, 14336, 4096], P('grp', 'tp'), may hold values from -0.046875 to 0.046875
Outputs:
- layer_out: bfloat16 [2048, 4096], P('tp', 'grp')
Inputs may be any that keep to these rules, and one draw needn't show every extreme that they name: `domain_ids`: in each aligned block of 128 positions (those of one index of tp) no domain is named by more than 32 positions, and in some block one domain is named by exactly 32. `expert_domain`: A permutation: every domain is served by exactly one stored expert.
All inputs are finite; a program needn't handle non-finite values.
Results may differ from a plain program's by a relative error of at most 0.017.
Values may be sent and summed in bfloat16 or wider, within the bound.
A program may use at most 128 MiB of HBM per device.

v0:
```python
import math

import jax
import jax.numpy as jnp
from jax import lax
from jax.sharding import PartitionSpec as P

HD = 64


NEG_FILL = -1e30


def shards(
    tokens_in,
    queries,
    keys_all,
    values_all,
    out_proj,
    domain_ids,
    expert_domain,
    gate_proj,
    up_proj,
    down_proj,
):
    rows_here = queries.shape[0]
    feat_width = queries.shape[1]
    heads_here = feat_width // HD
    model_width = out_proj.shape[1]
    groups = lax.axis_size("grp")
    shard_id = lax.axis_index("tp")
    group_id = lax.axis_index("grp")
    experts_all = expert_domain.shape[0]
    experts_here = gate_proj.shape[0]
    capacity = rows_here // 4
    score_scale = 1.0 / math.sqrt(HD)
    query_heads = queries.reshape(rows_here, heads_here, HD)
    query_pos = shard_id * rows_here + jnp.arange(rows_here)
    key_rows = lax.all_gather(keys_all, "tp", axis=0, tiled=True)
    value_rows = lax.all_gather(values_all, "tp", axis=0, tiled=True)
    row_count = key_rows.shape[0]
    key_heads = key_rows.reshape(row_count, heads_here, HD)
    value_heads = value_rows.reshape(row_count, heads_here, HD)
    scores = (
        jnp.einsum("qhd,khd->hqk", query_heads, key_heads, preferred_element_type=jnp.float32)
        * score_scale
    )
    visible = jnp.arange(row_count)[None, :] <= query_pos[:, None]
    scores = jnp.where(visible[None], scores, NEG_FILL)
    row_max = jnp.full((heads_here, rows_here), NEG_FILL, jnp.float32)
    new_max = jnp.maximum(row_max, jnp.max(scores, axis=2))
    weights = jnp.where(visible[None], jnp.exp(scores - new_max[:, :, None]), 0.0)
    row_sum = jnp.sum(weights, axis=2)
    weights_low = weights.astype(jnp.bfloat16)
    acc_out = jnp.einsum(
        "hqk,khd->hqd", weights_low, value_heads, preferred_element_type=jnp.float32
    )
    row_max, row_sum, acc_out = (new_max, row_sum, acc_out)
    attended = (
        (acc_out / row_sum[:, :, None])
        .transpose(1, 0, 2)
        .reshape(rows_here, feat_width)
        .astype(jnp.bfloat16)
    )
    attn_part = jnp.dot(attended, out_proj, preferred_element_type=jnp.float32)
    slice_width = tokens_in.shape[1]
    carried = lax.dynamic_update_slice_in_dim(
        jnp.zeros((rows_here, model_width), jnp.float32),
        tokens_in.astype(jnp.float32),
        group_id * slice_width,
        1,
    )
    mixed_term = attn_part + carried
    labels_here = domain_ids[:, 0]
    domain_hit = expert_domain[None, :] == labels_here[:, None]
    rank_of = jnp.cumsum(domain_hit.astype(jnp.int32), axis=0) - 1
    slot_of = jnp.sum(jnp.where(domain_hit, rank_of, 0), axis=1)
    placed = domain_hit.T[:, None, :] & (
        slot_of[None, None, :] == jnp.arange(capacity)[None, :, None]
    )
    by_section = (
        placed.reshape(groups, experts_here, capacity, rows_here)
        .transpose(0, 2, 1, 3)
        .reshape(experts_all * capacity, rows_here)
    )
    source_row = jnp.sum(
        jnp.where(by_section, jnp.arange(rows_here, dtype=jnp.int32)[None, :], 0), axis=1
    )
    slot_live = jnp.any(by_section, axis=1).astype(jnp.float32)
    section_sum = lax.psum_scatter(
        jnp.take(mixed_term, source_row, axis=0) * slot_live[:, None],
        "grp",
        scatter_dimension=0,
        tiled=True,
    )
    section_rows = section_sum.astype(jnp.bfloat16).reshape(capacity, experts_here, model_width)
    row_block = lax.all_gather(section_rows, "tp", axis=0, tiled=True)
    gate_act = jnp.einsum("red,edf->ref", row_block, gate_proj, preferred_element_type=jnp.float32)
    up_act = jnp.einsum("red,edf->ref", row_block, up_proj, preferred_element_type=jnp.float32)
    activated = (jax.nn.silu(gate_act) * up_act).astype(jnp.bfloat16)
    part_out = jnp.einsum("ref,efd->red", activated, down_proj, preferred_element_type=jnp.float32)
    total_sum = lax.psum(part_out, "tp")
    own_sum = lax.dynamic_slice_in_dim(total_sum, shard_id * capacity, capacity, 0)
    finished = (section_rows.astype(jnp.float32) + own_sum).astype(jnp.bfloat16)
    returned = lax.all_to_all(finished, "grp", split_axis=2, concat_axis=1, tiled=True)
    unplace = (
        placed.transpose(1, 0, 2).reshape(capacity * experts_all, rows_here).astype(jnp.bfloat16)
    )
    flat_rows = returned.reshape(capacity * experts_all, returned.shape[2])
    return jnp.einsum("rt,rd->td", unplace, flat_rows, preferred_element_type=jnp.float32).astype(
        jnp.bfloat16
    )


def solution(mesh):
    in_specs = (
        P("tp", "grp"),
        P("tp", "grp"),
        P("tp", "grp"),
        P("tp", "grp"),
        P("grp", None),
        P("tp", None),
        P(),
        P("grp", None, "tp"),
        P("grp", None, "tp"),
        P("grp", "tp", None),
    )
    out_specs = P("tp", "grp")
    return jax.shard_map(shards, mesh=mesh, in_specs=in_specs, out_specs=out_specs, check_vma=False)
```

profile of v0, /device:TPU:0, one launch (start us, length us, event | category | flops | bytes accessed | tf_op | source)
XLA Modules:
  0.0 498.4 jit_solution(7628040514024122582)
XLA Ops:
  6.5 0.7 all-gather.5.cloned.1.call-update
  7.3 0.7 all-gather.7.cloned.1.call-update
  8.1 0.8 compare_convert_fusion
  9.0 0.8 fusion.39
  9.8 0.8 broadcast_compare_fusion
  11.0 1.0 copy.26
  12.6 33.0 %all-gather.5.cloned.1.call-done = bf16[2048,512]{1,0:T(8,128)(2,1)} async-done(((bf16[128,512]{1,0:T(8,128)(2,1)}), bf16[2048,512]{1,0:T(8,128)(2,1)}) %all-gather.5.cloned.1.call-update) | async-done | bytes 2097168 | tf_op jit(solution)/shard_map/all_gather | solution.py:39
  45.6 2.9 copy.27
  48.5 1.7 fusion
  50.2 3.2 copy-done
  53.5 2.5 fusion.10
  55.9 25.4 %all-gather.7.cloned.1.call-done = bf16[2048,512]{1,0:T(8,128)(2,1)} async-done(((bf16[128,512]{1,0:T(8,128)(2,1)}), bf16[2048,512]{1,0:T(8,128)(2,1)}) %all-gather.7.cloned.1.call-update) | async-done | bytes 2097168 | tf_op jit(solution)/shard_map/all_gather | solution.py:40
  81.3 2.9 copy.28
  84.3 5.8 %fusion.30 = bf16[128,8,64]{0,2,1:T(8,128)(2,1)S(1)} fusion(bf16[2048,8,64]{0,2,1:T(8,128)(2,1)S(1)} %bitcast.94, f32[8,128,2048]{2,1,0:T(8,128)} %copy-done, f32[8,128]{1,0:T(8,128)S(1)} %broadcast_maximum_fusion, pred[128,2048]{1,0:T(8,128)(4,1)S(1)} %iota_compare_fusion, f32[128,8]{0,1:T(8,128)S(1)} %bitcast.100), kind=kOutput, calls=%fused_computation.27 | convolution fusion | flops 279052288 | bytes 10887168 | tf_op jit(solution)/shard_map/hqk,khd->hqd/dot_general | solution.py:55
  90.1 0.7 fusion.46
  91.0 3.8 gather_fusion
  94.8 4.9 select_multiply_fusion
  99.8 84.7 %reduce-scatter.2.cloned.1.call-done = f32[32,4096]{1,0:T(8,128)} async-done(((f32[256,4096]{1,0:T(8,128)}), f32[32,4096]{1,0:T(8,128)}) %reduce-scatter.2.cloned.1.call-update) | async-done | bytes 524304 | tf_op jit(solution)/shard_map/reduce_scatter | solution.py:90
  184.5 1.8 convert_element_type.51
  186.5 36.0 %all-gather.9.cloned.1.call-done = bf16[512,4096]{1,0:T(8,128)(2,1)} async-done(((bf16[32,4096]{1,0:T(8,128)(2,1)}), bf16[512,4096]{1,0:T(8,128)(2,1)}) %all-gather.9.cloned.1.call-update) | async-done | bytes 4194320 | tf_op jit(solution)/shard_map/all_gather | solution.py:97
  222.6 9.8 %fusion.5 = f32[512,896]{1,0:T(8,128)S(1)} fusion(bf16[512,4096]{1,0:T(8,128)(2,1)} %all-gather.9.cloned.1.call-done, bf16[1,4096,896]{2,1,0:T(8,128)(2,1)} %param.17), kind=kOutput, calls=%fused_computation.8 | convolution fusion | flops 3758096384 | bytes 13369344 | tf_op jit(solution)/shard_map/red,edf->ref/dot_general | solution.py:98
  232.4 16.9 %fusion.7 = f32[512,1,4096]{2,0,1:T(8,128)} fusion(bf16[1,896,4096]{2,1,0:T(8,128)(2,1)} %param.19, bf16[512,4096]{1,0:T(8,128)(2,1)} %all-gather.9.cloned.1.call-done, bf16[1,4096,896]{2,1,0:T(8,128)(2,1)} %param.18, f32[512,896]{1,0:T(8,128)S(1)} %fusion.5), kind=kOutput, calls=%fused_computation.10 | convolution fusion | flops 7518945280 | bytes 29097984 | tf_op jit(solution)/shard_map/ref,efd->red/dot_general | solution.py:101
  249.3 195.0 %all-reduce.2.cloned.1.call-done = f32[512,1,4096]{2,0,1:T(8,128)} async-done(((f32[512,1,4096]{2,0,1:T(8,128)}), f32[512,1,4096]{2,0,1:T(8,128)}) %all-reduce.2.cloned.1.call-update) | async-done | bytes 8388624 | tf_op jit(solution)/shard_map/psum | solution.py:102
  444.3 1.1 fusion.35
  445.4 2.8 copy.29
  448.1 0.5 broadcast.103
  448.7 22.6 %reduce.2 = bf16[4096,32]{1,0:T(8,128)(2,1)S(1)} reduce(bf16[4096,1,32]{2,1,0:T(2,128)(2,1)S(1)} %bitcast.93, bf16[]{:T(256)} %broadcast.103), dimensions={1}, to_apply=%bitcast.81.reduce_sub_computation | reduce | bytes 524290
  471.3 1.0 reshape.200
  472.3 15.1 %all_to_all.4 = bf16[8,2,8192]{2,1,0:T(2,128)(2,1)S(1)} all-to-all(bf16[8,2,8192]{2,1,0:T(2,128)(2,1)S(1)} %reshape.200), channel_id=1, replica_groups=mesh['grp'=8,'tp'=16] {'grp'}, dimensions={0} | all-to-all | bytes 524288 | tf_op jit(solution)/shard_map/all_to_all | solution.py:105
  487.4 1.4 reshape.201
  488.7 2.1 copy.30
  491.0 0.9 convolution_convert_fusion
  (31 shorter events, 1.8 us)
Async XLA Ops:
  6.5 39.1 %all-gather.5.cloned.1.call-start = ((), (), s32[]{:S(2)}) async-start(), calls=%async_computation.2 | async-start | bytes 2228224 | tf_op jit(solution)/shard_map/all_gather | solution.py:39
  7.3 74.1 %all-gather.7.cloned.1.call-start = ((), (), s32[]{:S(2)}) async-start(), calls=%async_computation.3 | async-start | bytes 2228224 | tf_op jit(solution)/shard_map/all_gather | solution.py:40
  8.0 176.5 %reduce-scatter.2.cloned.1.call-start = ((), (), s32[]{:S(2)}) async-start(), calls=%async_computation.4 | async-start | bytes 4718592 | tf_op jit(solution)/shard_map/reduce_scatter | solution.py:90
  50.2 3.2 copy-start
  84.2 5.8 %copy-start.1 = (bf16[512,4096]{1,0:T(8,128)(2,1)S(1)}, bf16[512,4096]{1,0:T(8,128)(2,1)}, u32[]{:S(2)}) copy-start(bf16[512,4096]{1,0:T(8,128)(2,1)} %param.14) | copy-start | bytes 12582916
  90.1 0.9 copy-start.3
  99.8 122.8 %all-gather.9.cloned.1.call-start = ((), (), s32[]{:S(2)}) async-start(), calls=%async_computation.6 | async-start | bytes 4456448 | tf_op jit(solution)/shard_map/all_gather | solution.py:97
  186.3 258.0 %all-reduce.2.cloned.1.call-start = ((), (), s32[]{:S(2)}) async-start(), calls=%async_computation.5 | async-start | bytes 16777216 | tf_op jit(solution)/shard_map/psum | solution.py:102
  249.3 195.0 %copy-start.2 = (f32[32,4096]{1,0:T(8,128)S(1)}, f32[32,4096]{1,0:T(8,128)}, u32[]{:S(2)}) copy-start(f32[32,4096]{1,0:T(8,128)} %reduce-scatter.2.cloned.1.call-done) | copy-start | bytes 1572868
Sparse Core Ops, SparseCore 0:
  9.1 36.4 all-gather.4
  47.3 33.9 all-gather.6
  99.9 84.5 reduce-scatter.1
  186.4 36.0 all-gather.8
  249.4 194.8 all-reduce.1
where the time goes:
time: 499 us; the launch traced here: 498 us
  waiting for transfers between devices  376 us (75%)
  other arithmetic  36.1 us (7%)
  matrix products  35.8 us (7%)
  local copies, waits for them, and re-layouts  22.1 us (4%)
  blocking collectives  15.1 us (3%)
  between operations  13.3 us (3%)
    psum x1, waiting for transfers between devices, shards(): total_sum = lax.psum(part_out, 'tp')  195 us
    reduce_scatter x1, waiting for transfers between devices, shards(): lax.psum_scatter(jnp.take(mixed_term, source_row, axis=0) * slot_live[:,...  84.7 us
    all_gather x1, waiting for transfers between devices, shards(): row_block = lax.all_gather(section_rows, 'tp', axis=0, tiled=True)  36 us
    all_gather x1, waiting for transfers between devices, shards(): key_rows = lax.all_gather(keys_all, 'tp', axis=0, tiled=True)  33 us
    all_gather x1, waiting for transfers between devices, shards(): value_rows = lax.all_gather(values_all, 'tp', axis=0, tiled=True)  25.4 us
    unnamed x1, other arithmetic  22.6 us
    dot_general x1, matrix products, shards(): jnp.einsum('ref,efd->red', activated, down_proj, preferred_element_type=j...  16.9 us
    all_to_all x1, blocking collectives, shards(): lax.all_to_all(finished, 'grp', split_axis=2, concat_axis=1, tiled=True)  15.1 us
  transfers between devices with their start and end apart: 5, of which 5 were waited for; matrix products, arithmetic and copies ran while one was open for 2% of the time, Pallas kernels for 0%

commit v1 on v0

v1 whole, which is shorter than its diff:
```python
import functools
import math

import jax
import jax.numpy as jnp
from jax import lax
from jax.experimental import pallas as pl
from jax.experimental.pallas import tpu as pltpu
from jax.sharding import PartitionSpec as P

HD = 64
NEG_FILL = -1e30
LANES = 128
MESH = pl.DeviceIdType.MESH
BF16 = jnp.bfloat16
F32 = jnp.float32


def slot(dy, dx, dc):
    return dc * 8 + dy * 2 + dx


class Links:
    def __init__(self, send_sems, recv_sems):
        t = lax.axis_index("tp")
        self.t = t
        self.g = lax.axis_index("grp")
        self.up = lax.rem(t + 4, 16)
        self.down = lax.rem(t + 12, 16)
        self.over = t + 2 - 4 * lax.rem(lax.div(t, 2), 2)
        self.twin = t + 1 - 2 * lax.rem(t, 2)
        self.send_sems, self.recv_sems = send_sems, recv_sems
        self.started = []

    def greet(self):
        barrier = pltpu.get_barrier_semaphore()
        for to in (self.up, self.down, self.over, self.twin):
            pl.semaphore_signal(
                barrier, inc=1, device_id={"tp": to, "grp": self.g}, device_id_type=MESH
            )
        for i in range(1, 8):
            pl.semaphore_signal(
                barrier,
                inc=1,
                device_id={"tp": self.t, "grp": lax.rem(self.g + i, 8)},
                device_id_type=MESH,
            )
        pl.semaphore_wait(barrier, 11)

    def send(self, src, dst, tp=None, grp=None):
        n = len(self.started)
        copy = pltpu.make_async_remote_copy(
            src_ref=src,
            dst_ref=dst,
            send_sem=self.send_sems.at[n],
            recv_sem=self.recv_sems.at[n],
            device_id={
                "tp": self.t if tp is None else tp,
                "grp": self.g if grp is None else grp,
            },
            device_id_type=MESH,
        )
        copy.start()
        self.started.append(copy)
        return copy

    def drain(self):
        for copy in self.started:
            copy.wait_send()


def gather(links, piece, part, whole):
    up, down, over, twin = links.up, links.down, links.over, links.twin
    own, west = slot(0, 0, 0), slot(0, 1, 0)
    below, above, far = slot(3, 0, 0), slot(1, 0, 0), slot(2, 0, 0)
    w_below, w_above, w_far = slot(3, 1, 0), slot(1, 1, 0), slot(2, 1, 0)
    shared = []

    def share(s):
        for ref, to in zip(whole(s), whole(s + 8)):
            shared.append(links.send(ref, to, tp=twin))

    def move(s, d, h, to, side=None):
        if side is None:
            return links.send(piece(s, h), piece(d, h), tp=to)
        return links.send(part(s, h, side), part(d, h, side), tp=to)

    a = move(own, west, 0, over)
    b = move(own, below, 0, up)
    c = move(own, above, 0, down)
    d = move(own, below, 1, up)
    e = move(own, above, 1, down)
    f = move(own, west, 1, over)
    share(own)
    a.wait_recv()
    g = move(west, w_below, 0, up)
    h = move(west, w_above, 0, down)
    b.wait_recv()
    i = move(below, far, 0, up, 0)
    c.wait_recv()
    j = move(above, far, 0, down, 1)
    d.wait_recv()
    k = move(below, far, 1, up, 0)
    l = move(below, w_below, 1, over)
    share(below)
    e.wait_recv()
    m = move(above, far, 1, down, 1)
    n = move(above, w_above, 1, over)
    share(above)
    f.wait_recv()
    share(west)
    g.wait_recv()
    o = move(w_below, w_far, 0, up, 0)
    h.wait_recv()
    p = move(w_above, w_far, 0, down, 1)
    i.wait_recv()
    j.wait_recv()
    k.wait_recv()
    m.wait_recv()
    q = move(far, w_far, 1, over)
    share(far)
    l.wait_recv()
    share(w_below)
    n.wait_recv()
    share(w_above)
    o.wait_recv()
    p.wait_recv()
    q.wait_recv()
    share(w_far)
    for copy in shared:
        copy.wait_recv()


def mix_kernel(
    q_ref, k_ref, v_ref, tok_ref, place_ref, proj_ref,
    mixed_ref, rows_ref,
    k_all, v_all, proj, bias, att, part_out, part_in, disp, rows,
    send_sems, recv_sems, proj_sem,
):
    links = Links(send_sems, recv_sems)
    n_rows = q_ref.shape[0]
    width = q_ref.shape[1]
    cap = disp.shape[1]
    half = n_rows // 2
    fetch = pltpu.make_async_copy(proj_ref, proj, proj_sem)
    fetch.start()
    k_all[0:n_rows, :] = k_ref[...]
    v_all[0:n_rows, :] = v_ref[...]
    links.greet()

    def piece(s, h):
        return (k_all, v_all)[h].at[pl.ds(s * n_rows, n_rows)]

    def part(s, h, side):
        return (k_all, v_all)[h].at[pl.ds(s * n_rows + side * half, half)]

    gather(links, piece, part, lambda s: (piece(s, 0), piece(s, 1)))

    n_keys = k_all.shape[0]
    t = links.t
    y, x, core = lax.div(t, 4), lax.rem(lax.div(t, 2), 2), lax.rem(t, 2)
    for s in range(16):
        dc, dy, dx = s // 8, (s % 8) // 2, s % 2
        if s == 0:
            row = lax.broadcasted_iota(jnp.int32, (n_rows, n_rows), 0)
            col = lax.broadcasted_iota(jnp.int32, (n_rows, n_rows), 1)
            bias[:, 0:n_rows] = jnp.where(col <= row, 0.0, NEG_FILL)
        else:
            from_y = lax.rem(y + dy, 4)
            from_x = x + dx - 2 * x * dx
            from_core = core + dc - 2 * core * dc
            hidden = (from_y * 4 + from_x * 2 + from_core > t).astype(F32)
            bias[:, s * n_rows : (s + 1) * n_rows] = jnp.full(
                (n_rows, n_rows), NEG_FILL, F32
            ) * hidden

    lane = lax.broadcasted_iota(jnp.int32, (n_rows, LANES), 1)
    low = lane < HD
    log2_scale = math.log2(math.e) / math.sqrt(HD)

    @pl.loop(0, width // LANES)
    def _(p):
        cols = pl.ds(pl.multiple_of(p * LANES, LANES), LANES)
        q_pair = q_ref[:, cols]
        zero = jnp.zeros_like(q_pair)
        q_two = jnp.concatenate([jnp.where(low, q_pair, zero), jnp.where(low, zero, q_pair)], 0)
        s = lax.dot_general(
            q_two, k_all[:, cols], (((1,), (1,)), ((), ())), preferred_element_type=F32
        )
        s = s + jnp.concatenate([bias[...], bias[...]], 0)
        top = jnp.max(s, axis=1, keepdims=True)
        w = jnp.exp2((s - top) * log2_scale)
        total = jnp.sum(w, axis=1, keepdims=True)
        o = jnp.dot(w.astype(BF16), v_all[:, cols], preferred_element_type=F32) / total
        att[:, cols] = jnp.where(low, o[0:n_rows], o[n_rows:]).astype(BF16)

    fetch.wait()
    sums = []
    for i in [1, 2, 3, 4, 5, 6, 7, 0]:
        to = lax.rem(links.g + i, 8)
        cols = pl.ds(pl.multiple_of(to * width, width), width)
        term = jnp.dot(att[...], proj[:, cols], preferred_element_type=F32)
        if i == 0:
            total = term + tok_ref[...].astype(F32)
        else:
            part_out[i] = term.astype(BF16)
            sums.append(links.send(part_out.at[i], part_in.at[i], grp=to))
    for i in range(1, 8):
        sums[i - 1].wait_recv()
        total = total + part_in[i].astype(F32)
    mixed = total.astype(BF16)
    mixed_ref[...] = mixed

    mine = pl.ds(pl.multiple_of(links.g * width, width), width)
    moved = []
    for i in [1, 2, 3, 4, 5, 6, 7, 0]:
        to = lax.rem(links.g + i, 8)
        take = place_ref[pl.ds(pl.multiple_of(to * cap, cap), cap), :]
        chosen = jnp.dot(take, mixed, preferred_element_type=F32).astype(BF16)
        if i == 0:
            rows[:, mine] = chosen
        else:
            disp[i] = chosen
            moved.append(links.send(disp.at[i], rows.at[:, mine], grp=to))
    for copy in moved:
        copy.wait_recv()
    rows_ref[...] = rows[...]
    links.drain()


def expert_kernel(
    rows_ref, gate_ref, up_ref, down_ref, unplace_ref, mixed_ref,
    out_ref,
    x_all, gate_up, down, act,
    own_sum, core_out, core_in, y_out, y_in, n_out, n_in, x_out, x_in, fin_out, fin_in,
    send_sems, recv_sems, load_sems,
):
    links = Links(send_sems, recv_sems)
    cap, width = rows_ref.shape
    hidden = act.shape[1]
    tiles = hidden // LANES
    n_rows = 16 * cap
    lane_rows = 8 * cap
    chunk = width // 8
    half_chunk = chunk // 2
    loads = []
    for j in range(tiles):
        for ref, at in ((gate_ref, 2 * j), (up_ref, 2 * j + 1)):
            load = pltpu.make_async_copy(
                ref.at[0, :, pl.ds(j * LANES, LANES)],
                gate_up.at[:, pl.ds(at * LANES, LANES)],
                load_sems.at[at],
            )
            load.start()
            loads.append(load)
    load_down = pltpu.make_async_copy(down_ref.at[0], down, load_sems.at[2 * tiles])
    load_down.start()
    x_all[0:cap, :] = rows_ref[...]
    links.greet()

    def piece(s, h):
        return x_all.at[pl.ds(s * cap, cap), pl.ds(h * (width // 2), width // 2)]

    def part(s, h, side):
        return x_all.at[
            pl.ds(s * cap, cap), pl.ds(h * (width // 2) + side * (width // 4), width // 4)
        ]

    gather(links, piece, part, lambda s: (x_all.at[pl.ds(s * cap, cap)],))
    for load in loads:
        load.wait()

    @pl.loop(0, tiles)
    def _(j):
        w = gate_up[:, pl.ds(pl.multiple_of(j * 2 * LANES, 2 * LANES), 2 * LANES)]
        for m in range(2):
            at = pl.ds(m * lane_rows, lane_rows)
            both = jnp.dot(x_all[at, :], w, preferred_element_type=F32)
            gate, lift = both[:, :LANES], both[:, LANES:]
            act[at, pl.ds(pl.multiple_of(j * LANES, LANES), LANES)] = (
                gate / (1.0 + jnp.exp(-gate)) * lift
            ).astype(BF16)

    load_down.wait()

    copies = [dict() for _ in range(8)]

    def start(i):
        to = lax.rem(links.g + i, 8)
        cols = pl.ds(pl.multiple_of(to * chunk, chunk), chunk)
        core_out[i] = jnp.dot(
            act[lane_rows:, :], down[:, cols], preferred_element_type=F32
        ).astype(BF16)
        copies[i]["core"] = links.send(core_out.at[i], core_in.at[i], tp=links.twin)
        own_sum[i] = jnp.dot(act[0:lane_rows, :], down[:, cols], preferred_element_type=F32)

    def core_sum(i):
        copies[i]["core"].wait_recv()
        own_sum[i] = own_sum[i] + core_in[i].astype(F32)

    def y_far(i, n):
        rows = pl.ds(2 * n, n)
        y_out[i, 0, 0:n] = own_sum[i, rows, 0:half_chunk].astype(BF16)
        y_out[i, 1, 0:n] = own_sum[i, rows, half_chunk:].astype(BF16)
        for s, to in ((0, links.up), (1, links.down)):
            copies[i]["far", s] = links.send(
                y_out.at[i, s, pl.ds(0, n)], y_in.at[i, s, pl.ds(0, n)], tp=to
            )

    def y_near(i, n):
        for s in range(2):
            copies[i]["far", s].wait_recv()
        left = own_sum[i, n : 2 * n, 0:half_chunk] + y_in[i, 0, 0:n].astype(F32)
        n_out[i, 0, 0:n, 0:half_chunk] = left.astype(BF16)
        n_out[i, 0, 0:n, half_chunk:] = own_sum[i, n : 2 * n, half_chunk:].astype(BF16)
        copies[i]["near", 0] = links.send(
            n_out.at[i, 0, pl.ds(0, n)], n_in.at[i, 0, pl.ds(0, n)], tp=links.up
        )
        right = own_sum[i, 3 * n : 4 * n, half_chunk:] + y_in[i, 1, 0:n].astype(F32)
        n_out[i, 1, 0:n, 0:half_chunk] = own_sum[i, 3 * n : 4 * n, 0:half_chunk].astype(BF16)
        n_out[i, 1, 0:n, half_chunk:] = right.astype(BF16)
        copies[i]["near", 1] = links.send(
            n_out.at[i, 1, pl.ds(0, n)], n_in.at[i, 1, pl.ds(0, n)], tp=links.down
        )

    def y_sum(i, n):
        for s in range(2):
            copies[i]["near", s].wait_recv()
        return own_sum[i, 0:n] + n_in[i, 0, 0:n].astype(F32) + n_in[i, 1, 0:n].astype(F32)

    def x_send(i, n):
        copies[i]["x"] = links.send(
            x_out.at[i, pl.ds(0, n)], x_in.at[i, pl.ds(0, n)], tp=links.over
        )

    mine = pl.ds(pl.multiple_of(links.g * cap, cap), cap)

    def finish(i, total):
        if i == 0:
            fin_in[mine, :] = total.astype(BF16)
        else:
            fin_out[i] = total.astype(BF16)
            copies[i]["fin"] = links.send(
                fin_out.at[i], fin_in.at[mine], grp=lax.rem(links.g + i, 8)
            )

    def stage(i, step):
        y_first = i % 2 == 0
        if step == 0:
            start(i)
        elif step == 1:
            core_sum(i)
            if y_first:
                y_far(i, 2 * cap)
            else:
                for b in range(4):
                    x_out[i, b * cap : (b + 1) * cap] = own_sum[
                        i, (2 * b + 1) * cap : (2 * b + 2) * cap
                    ].astype(BF16)
                x_send(i, 4 * cap)
        elif step == 2:
            if y_first:
                y_near(i, 2 * cap)
            else:
                copies[i]["x"].wait_recv()
                for b in range(4):
                    own_sum[i, b * cap : (b + 1) * cap] = own_sum[
                        i, 2 * b * cap : (2 * b + 1) * cap
                    ] + x_in[i, b * cap : (b + 1) * cap].astype(F32)
                y_far(i, cap)
        elif step == 3:
            if y_first:
                total = y_sum(i, 2 * cap)
                own_sum[i, 0:cap] = total[0:cap]
                x_out[i, 0:cap] = total[cap:].astype(BF16)
                x_send(i, cap)
            else:
                y_near(i, cap)
        else:
            if y_first:
                copies[i]["x"].wait_recv()
                finish(i, own_sum[i, 0:cap] + x_in[i, 0:cap].astype(F32))
            else:
                finish(i, y_sum(i, cap))

    order = [1, 2, 3, 4, 5, 6, 7, 0]
    for tick in range(8 + 4):
        for step in (4, 3, 2, 1, 0):
            at = tick - step
            if 0 <= at < 8:
                stage(order[at], step)
    for i in range(1, 8):
        copies[i]["fin"].wait_recv()
    out_ref[...] = (
        mixed_ref[...].astype(F32)
        + jnp.dot(unplace_ref[...], fin_in[...], preferred_element_type=F32)
    ).astype(BF16)
    links.drain()


def shards(
    tokens_in,
    queries,
    keys_all,
    values_all,
    out_proj,
    domain_ids,
    expert_domain,
    gate_proj,
    up_proj,
    down_proj,
):
    n_rows, width = queries.shape
    model = out_proj.shape[1]
    hidden = gate_proj.shape[2]
    cap = n_rows // 4
    chunk = model // 8
    vmem = pl.BlockSpec(memory_space=pltpu.VMEM)
    hbm = pl.BlockSpec(memory_space=pl.ANY)

    labels = domain_ids[:, 0]
    hit = expert_domain[:, None] == labels[None, :]
    rank = jnp.cumsum(hit.astype(jnp.int32), axis=1) - 1
    placed = hit[:, None, :] & (rank[:, None, :] == jnp.arange(cap)[None, :, None])
    place = placed.reshape(8 * cap, n_rows).astype(BF16)
    unplace = place.T

    mixed, rows = pl.pallas_call(
        mix_kernel,
        out_shape=(
            jax.ShapeDtypeStruct((n_rows, width), BF16),
            jax.ShapeDtypeStruct((cap, model), BF16),
        ),
        in_specs=[vmem] * 5 + [hbm],
        out_specs=(vmem, vmem),
        scratch_shapes=[
            pltpu.VMEM((16 * n_rows, width), BF16),
            pltpu.VMEM((16 * n_rows, width), BF16),
            pltpu.VMEM((width, model), BF16),
            pltpu.VMEM((n_rows, 16 * n_rows), F32),
            pltpu.VMEM((n_rows, width), BF16),
            pltpu.VMEM((8, n_rows, width), BF16),
            pltpu.VMEM((8, n_rows, width), BF16),
            pltpu.VMEM((8, cap, width), BF16),
            pltpu.VMEM((cap, model), BF16),
            pltpu.SemaphoreType.DMA((64,)),
            pltpu.SemaphoreType.DMA((64,)),
            pltpu.SemaphoreType.DMA,
        ],
        compiler_params=pltpu.CompilerParams(
            collective_id=0, has_side_effects=True, vmem_limit_bytes=56 * 2**20
        ),
        name="mix",
    )(queries, keys_all, values_all, tokens_in, place, out_proj)

    return pl.pallas_call(
        expert_kernel,
        out_shape=jax.ShapeDtypeStruct((n_rows, width), BF16),
        in_specs=[vmem, hbm, hbm, hbm, vmem, vmem],
        out_specs=vmem,
        scratch_shapes=[
            pltpu.VMEM((16 * cap, model), BF16),
            pltpu.VMEM((model, 2 * hidden), BF16),
            pltpu.VMEM((hidden, model), BF16),
            pltpu.VMEM((16 * cap, hidden), BF16),
            pltpu.VMEM((8, 8 * cap, chunk), F32),
            pltpu.VMEM((8, 8 * cap, chunk), BF16),
            pltpu.VMEM((8, 8 * cap, chunk), BF16),
            pltpu.VMEM((8, 2, 2 * cap, chunk // 2), BF16),
            pltpu.VMEM((8, 2, 2 * cap, chunk // 2), BF16),
            pltpu.VMEM((8, 2, 2 * cap, chunk), BF16),
            pltpu.VMEM((8, 2, 2 * cap, chunk), BF16),
            pltpu.VMEM((8, 4 * cap, chunk), BF16),
            pltpu.VMEM((8, 4 * cap, chunk), BF16),
            pltpu.VMEM((8, cap, chunk), BF16),
            pltpu.VMEM((8 * cap, chunk), BF16),
            pltpu.SemaphoreType.DMA((96,)),
            pltpu.SemaphoreType.DMA((96,)),
            pltpu.SemaphoreType.DMA((2 * (hidden // LANES) + 1,)),
        ],
        compiler_params=pltpu.CompilerParams(
            collective_id=1, has_side_effects=True, vmem_limit_bytes=56 * 2**20
        ),
        name="expert",
    )(rows, gate_proj, up_proj, down_proj, unplace, mixed)


def solution(mesh):
    in_specs = (
        P("tp", "grp"),
        P("tp", "grp"),
        P("tp", "grp"),
        P("tp", "grp"),
        P("grp", None),
        P("tp", None),
        P(),
        P("grp", None, "tp"),
        P("grp", None, "tp"),
        P("grp", "tp", None),
    )
    out_specs = P("tp", "grp")
    return jax.shard_map(shards, mesh=mesh, in_specs=in_specs, out_specs=out_specs, check_vma=False)
```

time: 499 us -> 136 us (0.27)
  waiting for transfers between devices: 376 us -> 0 us
  Pallas kernels: 0 us -> 132 us
  matrix products: 35.8 us -> 0 us
  other arithmetic: 36.1 us -> 1.06 us
  local copies, waits for them, and re-layouts: 22.1 us -> 2.63 us
  blocking collectives: 15.1 us -> 0 us
  between operations: 13.3 us -> 0.07 us
    psum x1 -> x0, waiting for transfers between devices: 195 us -> none  [shards(): total_sum = lax.psum(part_out, 'tp')]
    pallas_call x0 -> x2, Pallas kernels: none -> 132 us  [the longest x1 77.7 us: shards(): pl.pallas_call(expert_kernel, out_shape=jax.ShapeDtypeStruct((n_rows, wid...]
    all_gather x3 -> x0, waiting for transfers between devices: 94.4 us -> none  [the longest x1 36 us: shards(): row_block = lax.all_gather(section_rows, 'tp', axis=0, tiled=True)]
    reduce_scatter x1 -> x0, waiting for transfers between devices: 84.7 us -> none  [shards(): lax.psum_scatter(jnp.take(mixed_term, source_row, axis=0) * slot_live[:,...]
    dot_general x6 -> x0, matrix products: 35.8 us -> none  [the longest x1 16.9 us: shards(): jnp.einsum('ref,efd->red', activated, down_proj, preferred_element_type=j...]
    unnamed x1 -> x0, other arithmetic: 22.6 us -> none
    all_to_all x1 -> x0, blocking collectives: 15.1 us -> none  [shards(): lax.all_to_all(finished, 'grp', split_axis=2, concat_axis=1, tiled=True)]
    all_gather x2 -> x0, local copies, waits for them, and re-layouts: 5.85 us -> none  [the longest x1 2.93 us: shards(): key_rows = lax.all_gather(keys_all, 'tp', axis=0, tiled=True)]
  transfers between devices with their start and end apart: 5 -> 0, of which waited for: 5 -> 0; matrix products, arithmetic and copies ran while one was open for 2% -> 0% of each run, Pallas kernels for 0% -> 0%
where the time goes in v1:
time: 136 us
  Pallas kernels  132 us (97%)
  local copies, waits for them, and re-layouts  2.63 us (2%)
    pallas_call x1, Pallas kernels, shards(): pl.pallas_call(expert_kernel, out_shape=jax.ShapeDtypeStruct((n_rows, wid...  77.7 us
    pallas_call x1, Pallas kernels, shards(): pl.pallas_call(mix_kernel, out_shape=(jax.ShapeDtypeStruct((n_rows, width...  54.5 us

profile of v1, /device:TPU:0, one launch (start us, length us, event | category | flops | bytes accessed | tf_op | source)
XLA Modules:
  0.0 135.9 jit_solution(9602140648796202977)
XLA Ops:
  0.0 0.1 eq.50
  0.1 0.7 fusion
  0.8 0.3 reduce_window_sum.11
  1.1 0.1 copy.15
  1.3 0.1 copy.14
  1.4 0.0 copy-start
  1.4 0.7 copy.16.place_ref
  2.2 54.5 %mix.1 = (bf16[128,512]{1,0:T(8,128)(2,1)}, bf16[32,4096]{1,0:T(8,128)(2,1)}) custom-call(bf16[128,512]{1,0:T(8,128)(2,1)} %q_ref.1, bf16[128,512]{1,0:T(8,128)(2,1)} %k_ref.1, bf16[128,512]{1,0:T(8,128)(2,1)} %v_ref.1, bf16[128,512]{1,0:T(8,128)(2,1)} %tok_ref.1, bf16[256,128]{1,0:T(8,128)(2,1)} %copy.16.place_ref, bf16[512,4096]{1,0:T(8,128)(2,1)} %proj_ref.1), custom_call_target="tpu_custom_call" | custom-call | tf_op jit(solution)/shard_map/mix/pallas_call | solution.py:428
  56.7 0.0 copy-done
  56.7 77.7 %expert.1 = bf16[128,512]{1,0:T(8,128)(2,1)} custom-call(bf16[32,4096]{1,0:T(8,128)(2,1)} %get-tuple-element.7.rows_ref, bf16[1,4096,896]{2,1,0:T(8,128)(2,1)} %gate_ref.1, bf16[1,4096,896]{2,1,0:T(8,128)(2,1)} %up_ref.1, bf16[1,896,4096]{2,1,0:T(8,128)(2,1)} %down_ref.1, bf16[128,256]{1,0:T(8,128)(2,1)} %bitcast.4, bf16[128,512]{1,0:T(8,128)(2,1)} %get-tuple-element.8.mixed_ref), custom_call_target="tpu_custom_call" | custom-call | tf_op jit(solution)/shard_map/expert/pallas_call | solution.py:456
  134.3 1.6 %copy.18 = bf16[128,512]{1,0:T(8,128)(2,1)} copy(bf16[128,512]{1,0:T(8,128)(2,1)} %expert.1) | data formatting | bytes 262144
  (5 shorter events, 0.1 us)
Async XLA Ops:
  1.4 55.3 %copy-start = (bf16[256,128]{0,1:T(8,128)(2,1)}, bf16[256,128]{0,1:T(8,128)(2,1)S(1)}, u32[]{:S(2)}) copy-start(bf16[256,128]{0,1:T(8,128)(2,1)S(1)} %and_convert_fusion) | copy-start | bytes 196612

commit v2 on v1

v2 whole, which is shorter than its diff:
```python
import functools
import math

import jax
import jax.numpy as jnp
from jax import lax
from jax.experimental import pallas as pl
from jax.experimental.pallas import tpu as pltpu
from jax.sharding import PartitionSpec as P

HD = 64
NEG_FILL = -1e30
LANES = 128
MESH = pl.DeviceIdType.MESH
BF16 = jnp.bfloat16
F32 = jnp.float32


def slot(dy, dx, dc):
    return (0, 1, 3, 2)[dy] * 4 + dc * 2 + dx


def unslot(s):
    return (0, 1, 3, 2)[s // 4], s % 2, (s // 2) % 2


CHUNKS = (1, 2, 3, 4, 5, 6, 7, 0)
X_FIRST = (2, 6, 7)
STEPS = (
    (0, 0), (1, 0), (2, 0), (3, 0), (0, 1), (4, 0), (1, 1), (2, 1), (5, 0),
    (3, 1), (6, 0), (4, 1), (7, 0), (0, 2), (5, 1), (6, 1), (2, 2), (7, 1),
    (3, 2), (4, 2), (1, 2), (0, 3), (2, 3), (5, 2), (7, 2), (3, 3), (6, 2),
    (4, 3), (1, 3), (5, 3), (7, 3), (6, 3), (1, 4), (5, 4), (6, 4),
)


class Links:
    def __init__(self, send_sems, recv_sems):
        t = lax.axis_index("tp")
        self.t = t
        self.g = lax.axis_index("grp")
        self.up = lax.rem(t + 4, 16)
        self.down = lax.rem(t + 12, 16)
        self.over = t + 2 - 4 * lax.rem(lax.div(t, 2), 2)
        self.twin = t + 1 - 2 * lax.rem(t, 2)
        self.send_sems, self.recv_sems = send_sems, recv_sems
        self.started = []

    def greet(self):
        barrier = pltpu.get_barrier_semaphore()
        for to in (self.up, self.down, self.over, self.twin):
            pl.semaphore_signal(
                barrier, inc=1, device_id={"tp": to, "grp": self.g}, device_id_type=MESH
            )
        for i in range(1, 8):
            for to in (self.t, self.over):
                pl.semaphore_signal(
                    barrier,
                    inc=1,
                    device_id={"tp": to, "grp": lax.rem(self.g + i, 8)},
                    device_id_type=MESH,
                )
        pl.semaphore_wait(barrier, 18)

    def send(self, src, dst, tp=None, grp=None):
        n = len(self.started)
        copy = pltpu.make_async_remote_copy(
            src_ref=src,
            dst_ref=dst,
            send_sem=self.send_sems.at[n],
            recv_sem=self.recv_sems.at[n],
            device_id={
                "tp": self.t if tp is None else tp,
                "grp": self.g if grp is None else grp,
            },
            device_id_type=MESH,
        )
        copy.start()
        self.started.append(copy)
        return copy

    def drain(self):
        for copy in self.started:
            copy.wait_send()


def gather(links, piece, part, whole):
    up, down, over, twin = links.up, links.down, links.over, links.twin
    own, west = slot(0, 0, 0), slot(0, 1, 0)
    below, above, far = slot(3, 0, 0), slot(1, 0, 0), slot(2, 0, 0)
    w_below, w_above, w_far = slot(3, 1, 0), slot(1, 1, 0), slot(2, 1, 0)
    shared = {}

    def share(s):
        shared[s] = [links.send(ref, to, tp=twin) for ref, to in zip(whole(s), whole(s + 2))]

    def shared_here(*slots):
        for s in slots:
            for copy in shared[s]:
                copy.wait_recv()

    def move(s, d, h, to, side=None):
        if side is None:
            return links.send(piece(s, h), piece(d, h), tp=to)
        return links.send(part(s, h, side), part(d, h, side), tp=to)

    a = move(own, west, 0, over)
    d = move(own, below, 1, up)
    e = move(own, above, 1, down)
    b = move(own, below, 0, up)
    c = move(own, above, 0, down)
    f = move(own, west, 1, over)
    share(own)
    e.wait_recv()
    m = move(above, far, 1, down, 1)
    n = move(above, w_above, 1, over)
    d.wait_recv()
    k = move(below, far, 1, up, 0)
    l = move(below, w_below, 1, over)
    a.wait_recv()
    g = move(west, w_below, 0, up)
    h = move(west, w_above, 0, down)
    f.wait_recv()
    share(west)
    c.wait_recv()
    j = move(above, far, 0, down, 1)
    share(above)
    b.wait_recv()
    i = move(below, far, 0, up, 0)
    share(below)
    k.wait_recv()
    m.wait_recv()
    q = move(far, w_far, 1, over)
    n.wait_recv()
    h.wait_recv()
    p = move(w_above, w_far, 0, down, 1)
    share(w_above)
    g.wait_recv()
    o = move(w_below, w_far, 0, up, 0)
    shared_here(own, west, above, w_above)
    yield
    l.wait_recv()
    share(w_below)
    i.wait_recv()
    j.wait_recv()
    share(far)
    yield
    o.wait_recv()
    p.wait_recv()
    q.wait_recv()
    share(w_far)
    yield
    shared_here(below, w_below, far, w_far)


def mix(
    links, q_ref, k_ref, v_ref, tok_ref, place_ref,
    k_all, v_all, proj, bias, att, part_out, part_in, disp, x_all, fetch,
):
    n_rows, width = q_ref.shape
    cap = disp.shape[1]
    half = n_rows // 2

    def piece(s, h):
        return (k_all, v_all)[h].at[pl.ds(s * n_rows, n_rows)]

    def part(s, h, side):
        return (k_all, v_all)[h].at[pl.ds(s * n_rows + side * half, half)]

    t = links.t
    y, x, core = lax.div(t, 4), lax.rem(lax.div(t, 2), 2), lax.rem(t, 2)

    def set_bias():
        for s in range(16):
            dy, dx, dc = unslot(s)
            if s == 0:
                row = lax.broadcasted_iota(jnp.int32, (n_rows, n_rows), 0)
                col = lax.broadcasted_iota(jnp.int32, (n_rows, n_rows), 1)
                bias[:, 0:n_rows] = jnp.where(col <= row, 0.0, NEG_FILL)
            else:
                from_y = lax.rem(y + dy, 4)
                from_x = x + dx - 2 * x * dx
                from_core = core + dc - 2 * core * dc
                hidden = (from_y * 4 + from_x * 2 + from_core > t).astype(F32)
                bias[:, s * n_rows : (s + 1) * n_rows] = (
                    jnp.full((n_rows, n_rows), NEG_FILL, F32) * hidden
                )

    lane = lax.broadcasted_iota(jnp.int32, (n_rows, LANES), 1)
    low = lane < HD
    log2_scale = math.log2(math.e) / math.sqrt(HD)

    def attend():
        @pl.loop(0, width // LANES)
        def _(p):
            cols = pl.ds(pl.multiple_of(p * LANES, LANES), LANES)
            q_pair = q_ref[:, cols]
            zero = jnp.zeros_like(q_pair)
            q_two = jnp.concatenate([jnp.where(low, q_pair, zero), jnp.where(low, zero, q_pair)], 0)
            s = lax.dot_general(
                q_two, k_all[:, cols], (((1,), (1,)), ((), ())), preferred_element_type=F32
            )
            s = s + jnp.concatenate([bias[...], bias[...]], 0)
            top = jnp.max(s, axis=1, keepdims=True)
            w = jnp.exp2((s - top) * log2_scale)
            total = jnp.sum(w, axis=1, keepdims=True)
            o = jnp.dot(w.astype(BF16), v_all[:, cols], preferred_element_type=F32) / total
            att[:, cols] = jnp.where(low, o[0:n_rows], o[n_rows:]).astype(BF16)

    set_bias()
    for _ in gather(links, piece, part, lambda s: (piece(s, 0), piece(s, 1))):
        pass
    attend()

    fetch.wait()
    sums = []
    for i in (1, 2, 3, 4, 5, 6, 7, 0):
        to = lax.rem(links.g + i, 8)
        cols = pl.ds(pl.multiple_of(to * width, width), width)
        term = jnp.dot(att[...], proj[:, cols], preferred_element_type=F32)
        if i == 0:
            total = term + tok_ref[...].astype(F32)
        else:
            part_out[i] = term.astype(BF16)
            sums.append(links.send(part_out.at[i], part_in.at[i], grp=to))
    for i in range(1, 8):
        sums[i - 1].wait_recv()
        total = total + part_in[i].astype(F32)
    mixed = total.astype(BF16)

    mine = pl.ds(pl.multiple_of(links.g * width, width), width)
    moved = []
    for i in (1, 2, 3, 4, 5, 6, 7, 0):
        to = lax.rem(links.g + i, 8)
        take = place_ref[pl.ds(pl.multiple_of(to * cap, cap), cap), :]
        chosen = jnp.dot(take, mixed, preferred_element_type=F32).astype(BF16)
        if i == 0:
            x_all[0:cap, mine] = chosen
        else:
            disp[i] = chosen
            moved.append(links.send(disp.at[i], x_all.at[pl.ds(0, cap), mine], grp=to))
    for copy in moved:
        copy.wait_recv()
    return mixed


def experts(
    links, x_all, gate_up, down, act,
    own_sum, core_out, core_in, y_out, y_in, n_out, n_in, x_out, x_in, fin_out, fin_a, fin_b,
    loads, load_down,
):
    cap, width = x_all.shape[0] // 16, x_all.shape[1]
    tiles = act.shape[1] // LANES
    half_rows = 8 * cap
    chunk = width // 8
    half_chunk = chunk // 2

    def piece(s, h):
        return x_all.at[pl.ds(s * cap, cap), pl.ds(h * (width // 2), width // 2)]

    def part(s, h, side):
        return x_all.at[
            pl.ds(s * cap, cap), pl.ds(h * (width // 2) + side * (width // 4), width // 4)
        ]

    def hidden_units(m, first, last):
        at = pl.ds(m * half_rows, half_rows)

        @pl.loop(first, last)
        def _(j):
            w = gate_up[:, pl.ds(pl.multiple_of(j * 2 * LANES, 2 * LANES), 2 * LANES)]
            both = jnp.dot(x_all[at, :], w, preferred_element_type=F32)
            gate, lift = both[:, :LANES], both[:, LANES:]
            act[at, pl.ds(pl.multiple_of(j * LANES, LANES), LANES)] = (
                gate / (1.0 + jnp.exp(-gate)) * lift
            ).astype(BF16)

    done = 0
    for upto in gather(links, piece, part, lambda s: (x_all.at[pl.ds(s * cap, cap)],)):
        if done == 0:
            for load in loads:
                load.wait()
        upto = (3, 5, tiles)[done]
        hidden_units(0, (0, 3, 5)[done], upto)
        done += 1
    hidden_units(1, 0, tiles)
    load_down.wait()

    copies = [dict() for _ in range(8)]
    pair = 2 * cap
    near_up, near_down, far = (1, 2, 3)
    x_at = {i: n for n, i in enumerate(X_FIRST)}

    def start(i):
        to = lax.rem(links.g + i, 8)
        cols = pl.ds(pl.multiple_of(to * chunk, chunk), chunk)
        out = jnp.dot(act[...], down[:, cols], preferred_element_type=F32)
        for b in range(4):
            core_out[i, b * pair : (b + 1) * pair] = out[
                (2 * b + 1) * pair : (2 * b + 2) * pair
            ].astype(BF16)
        copies[i]["core"] = links.send(core_out.at[i], core_in.at[i], tp=links.twin)
        for b in range(4):
            own_sum[i, b * pair : (b + 1) * pair] = out[2 * b * pair : (2 * b + 1) * pair]

    def core_sum(i):
        copies[i]["core"].wait_recv()
        own_sum[i] = own_sum[i] + core_in[i].astype(F32)

    def y_far(i, n):
        rows = pl.ds(far * n, n)
        y_out[i, 0, 0:n] = own_sum[i, rows, 0:half_chunk].astype(BF16)
        y_out[i, 1, 0:n] = own_sum[i, rows, half_chunk:].astype(BF16)
        for s, to in ((0, links.up), (1, links.down)):
            copies[i]["far", s] = links.send(
                y_out.at[i, s, pl.ds(0, n)], y_in.at[i, s, pl.ds(0, n)], tp=to
            )

    def y_near(i, n):
        for s, at, to in ((0, near_up, links.up), (1, near_down, links.down)):
            copies[i]["far", s].wait_recv()
            block = own_sum[i, at * n : (at + 1) * n]
            left, right = block[:, 0:half_chunk], block[:, half_chunk:]
            passing = y_in[i, s, 0:n].astype(F32)
            left, right = (left + passing, right) if s == 0 else (left, right + passing)
            n_out[i, s, 0:n, 0:half_chunk] = left.astype(BF16)
            n_out[i, s, 0:n, half_chunk:] = right.astype(BF16)
            copies[i]["near", s] = links.send(
                n_out.at[i, s, pl.ds(0, n)], n_in.at[i, s, pl.ds(0, n)], tp=to
            )

    def y_sum(i, n):
        for s in range(2):
            copies[i]["near", s].wait_recv()
        return own_sum[i, 0:n] + n_in[i, 0, 0:n].astype(F32) + n_in[i, 1, 0:n].astype(F32)

    mine = pl.ds(pl.multiple_of(links.g * cap, cap), cap)

    def finish(i, total, side, into, tp):
        if i == 0 and tp is links.t:
            into[mine, :] = total.astype(BF16)
        else:
            at = pl.ds(side * cap, cap)
            fin_out[i, at] = total.astype(BF16)
            copies[i]["fin", side] = links.send(
                fin_out.at[i, at], into.at[mine], tp=tp, grp=lax.rem(links.g + i, 8)
            )

    def stage(i, step):
        if step == 0:
            start(i)
        elif i not in x_at:
            if step == 1:
                core_sum(i)
                y_far(i, pair)
            elif step == 2:
                y_near(i, pair)
            else:
                total = y_sum(i, pair)
                finish(i, total[cap:], 1, fin_b, links.over)
                finish(i, total[0:cap], 0, fin_a, links.t)
        elif step == 1:
            core_sum(i)
            for b in range(4):
                x_out[x_at[i], b * cap : (b + 1) * cap] = own_sum[
                    i, (2 * b + 1) * cap : (2 * b + 2) * cap
                ].astype(BF16)
            copies[i]["x"] = links.send(x_out.at[x_at[i]], x_in.at[x_at[i]], tp=links.over)
        elif step == 2:
            copies[i]["x"].wait_recv()
            for b in range(4):
                own_sum[i, b * cap : (b + 1) * cap] = own_sum[
                    i, 2 * b * cap : (2 * b + 1) * cap
                ] + x_in[x_at[i], b * cap : (b + 1) * cap].astype(F32)
            y_far(i, cap)
        elif step == 3:
            y_near(i, cap)
        else:
            finish(i, y_sum(i, cap), 0, fin_a, links.t)

    for i in X_FIRST:
        rows = pl.ds(pl.multiple_of(lax.rem(links.g + 8 - i, 8) * cap, cap), cap)
        fin_b[rows, :] = jnp.zeros((cap, chunk), BF16)
    for at, step in STEPS:
        stage(CHUNKS[at], step)
    for i in range(8):
        for side in range(2):
            if ("fin", side) in copies[i]:
                copies[i]["fin", side].wait_recv()


def layer_kernel(
    q_ref, k_ref, v_ref, tok_ref, place_ref, unplace_ref, proj_ref, gate_ref, up_ref, down_ref,
    mixed_ref, ffn_ref,
    k_all, v_all, proj, bias, att, part_out, part_in, disp,
    x_all, gate_up, down, act,
    own_sum, core_out, core_in, y_out, y_in, n_out, n_in, x_out, x_in, fin_out, fin_a, fin_b,
    send_sems, recv_sems, load_sems,
):
    links = Links(send_sems, recv_sems)
    n_rows = q_ref.shape[0]
    tiles = act.shape[1] // LANES
    fetch = pltpu.make_async_copy(proj_ref, proj, load_sems.at[2 * tiles + 1])
    load_down = pltpu.make_async_copy(down_ref.at[0], down, load_sems.at[2 * tiles])
    loads = []
    for j in range(tiles):
        for ref, at in ((gate_ref, 2 * j), (up_ref, 2 * j + 1)):
            loads.append(
                pltpu.make_async_copy(
                    ref.at[0, :, pl.ds(j * LANES, LANES)],
                    gate_up.at[:, pl.ds(at * LANES, LANES)],
                    load_sems.at[at],
                )
            )
    k_all[0:n_rows, :] = k_ref[...]
    v_all[0:n_rows, :] = v_ref[...]
    links.greet()
    for load in (fetch, *loads, load_down):
        load.start()
    mixed = mix(
        links, q_ref, k_ref, v_ref, tok_ref, place_ref,
        k_all, v_all, proj, bias, att, part_out, part_in, disp, x_all, fetch,
    )
    mixed_ref[...] = mixed
    experts(
        links, x_all, gate_up, down, act,
        own_sum, core_out, core_in, y_out, y_in, n_out, n_in, x_out, x_in, fin_out, fin_a, fin_b,
        loads, load_down,
    )
    fin = (fin_a[...].astype(F32) + fin_b[...].astype(F32)).astype(BF16)
    ffn_ref[...] = jnp.dot(unplace_ref[...], fin, preferred_element_type=F32)
    links.drain()


def shards(
    tokens_in,
    queries,
    keys_all,
    values_all,
    out_proj,
    domain_ids,
    expert_domain,
    gate_proj,
    up_proj,
    down_proj,
):
    n_rows, width = queries.shape
    model = out_proj.shape[1]
    hidden = gate_proj.shape[2]
    cap = n_rows // 4
    chunk = model // 8
    vmem = pl.BlockSpec(memory_space=pltpu.VMEM)
    hbm = pl.BlockSpec(memory_space=pl.ANY)

    labels = domain_ids[:, 0]
    hit = expert_domain[:, None] == labels[None, :]
    rank = jnp.cumsum(hit.astype(jnp.int32), axis=1) - 1
    placed = hit[:, None, :] & (rank[:, None, :] == jnp.arange(cap)[None, :, None])
    place = placed.reshape(8 * cap, n_rows).astype(BF16)

    mixed, ffn = pl.pallas_call(
        layer_kernel,
        out_shape=(
            jax.ShapeDtypeStruct((n_rows, width), BF16),
            jax.ShapeDtypeStruct((n_rows, width), F32),
        ),
        in_specs=[vmem] * 6 + [hbm] * 4,
        out_specs=(vmem, vmem),
        scratch_shapes=[
            pltpu.VMEM((16 * n_rows, width), BF16),
            pltpu.VMEM((16 * n_rows, width), BF16),
            pltpu.VMEM((width, model), BF16),
            pltpu.VMEM((n_rows, 16 * n_rows), F32),
            pltpu.VMEM((n_rows, width), BF16),
            pltpu.VMEM((8, n_rows, width), BF16),
            pltpu.VMEM((8, n_rows, width), BF16),
            pltpu.VMEM((8, cap, width), BF16),
            pltpu.VMEM((16 * cap, model), BF16),
            pltpu.VMEM((model, 2 * hidden), BF16),
            pltpu.VMEM((hidden, model), BF16),
            pltpu.VMEM((16 * cap, hidden), BF16),
            pltpu.VMEM((8, 8 * cap, chunk), F32),
            pltpu.VMEM((8, 8 * cap, chunk), BF16),
            pltpu.VMEM((8, 8 * cap, chunk), BF16),
            pltpu.VMEM((8, 2, 2 * cap, chunk // 2), BF16),
            pltpu.VMEM((8, 2, 2 * cap, chunk // 2), BF16),
            pltpu.VMEM((8, 2, 2 * cap, chunk), BF16),
            pltpu.VMEM((8, 2, 2 * cap, chunk), BF16),
            pltpu.VMEM((len(X_FIRST), 4 * cap, chunk), BF16),
            pltpu.VMEM((len(X_FIRST), 4 * cap, chunk), BF16),
            pltpu.VMEM((8, 2 * cap, chunk), BF16),
            pltpu.VMEM((8 * cap, chunk), BF16),
            pltpu.VMEM((8 * cap, chunk), BF16),
            pltpu.SemaphoreType.DMA((160,)),
            pltpu.SemaphoreType.DMA((160,)),
            pltpu.SemaphoreType.DMA((2 * (hidden // LANES) + 2,)),
        ],
        compiler_params=pltpu.CompilerParams(
            collective_id=0, has_side_effects=True, vmem_limit_bytes=62 * 2**20
        ),
        name="layer",
    )(
        queries, keys_all, values_all, tokens_in, place, place.T,
        out_proj, gate_proj, up_proj, down_proj,
    )
    return (mixed.astype(F32) + ffn).astype(BF16)


def solution(mesh):
    in_specs = (
        P("tp", "grp"),
        P("tp", "grp"),
        P("tp", "grp"),
        P("tp", "grp"),
        P("grp", None),
        P("tp", None),
        P(),
        P("grp", None, "tp"),
        P("grp", None, "tp"),
        P("grp", "tp", None),
    )
    out_specs = P("tp", "grp")
    return jax.shard_map(shards, mesh=mesh, in_specs=in_specs, out_specs=out_specs, check_vma=False)
```

time: 136 us -> 108 us (0.79)
  Pallas kernels: 132 us -> 104 us
  other arithmetic: 1.06 us -> 2.72 us
  local copies, waits for them, and re-layouts: 2.63 us -> 1.06 us
    pallas_call x2 -> x1, Pallas kernels: 132 us -> 104 us  [shards(): pl.pallas_call(layer_kernel, out_shape=(jax.ShapeDtypeStruct((n_rows, wid...]
    convert_element_type x0 -> x1, other arithmetic: none -> 1.67 us  [shards(): return (mixed.astype(F32) + ffn).astype(BF16)]
    unnamed x3 -> x2, local copies, waits for them, and re-layouts: 1.57 us -> 0.01 us
where the time goes in v2:
time: 108 us
  Pallas kernels  104 us (96%)
  other arithmetic  2.72 us (3%)
    pallas_call x1, Pallas kernels, shards(): pl.pallas_call(layer_kernel, out_shape=(jax.ShapeDtypeStruct((n_rows, wid...  104 us

profile of v2, /device:TPU:0, one launch (start us, length us, event | category | flops | bytes accessed | tf_op | source)
XLA Modules:
  0.0 108.1 jit_solution(1165854460377087999)
XLA Ops:
  0.0 0.1 eq.50
  0.1 0.7 fusion
  0.8 0.3 reduce_window_sum.11
  1.1 0.1 copy.15
  1.3 0.1 copy.14
  1.4 0.0 copy-start
  1.4 0.7 copy.16.place_ref
  2.2 0.0 copy-done
  2.2 104.3 %layer.1 = (bf16[128,512]{1,0:T(8,128)(2,1)}, f32[128,512]{1,0:T(8,128)}) custom-call(bf16[128,512]{1,0:T(8,128)(2,1)} %q_ref.1, bf16[128,512]{1,0:T(8,128)(2,1)} %k_ref.1, bf16[128,512]{1,0:T(8,128)(2,1)} %v_ref.1, bf16[128,512]{1,0:T(8,128)(2,1)} %tok_ref.1, bf16[256,128]{1,0:T(8,128)(2,1)} %copy.16.place_ref, bf16[128,256]{1,0:T(8,128)(2,1)} %bitcast.4, ...), custom_call_target="tpu_custom_call" | custom-call | tf_op jit(solution)/shard_map/layer/pallas_call | solution.py:461
  106.5 1.7 %add_convert_fusion = bf16[128,512]{1,0:T(8,128)(2,1)} fusion(f32[128,512]{1,0:T(8,128)} %get-tuple-element.8, bf16[128,512]{1,0:T(8,128)(2,1)} %get-tuple-element.7), kind=kLoop, calls=%fused_computation | loop fusion | flops 196608 | bytes 524288 | tf_op jit(solution)/shard_map/convert_element_type | solution.py:506
  (5 shorter events, 0.1 us)
Async XLA Ops:
  1.4 0.7 copy-start

commit v3 on v2

v3 whole, which is shorter than its diff:
```python
import functools
import math

import jax
import jax.numpy as jnp
from jax import lax
from jax.experimental import pallas as pl
from jax.experimental.pallas import tpu as pltpu
from jax.sharding import PartitionSpec as P

HD = 64
NEG_FILL = -1e30
LANES = 128
MESH = pl.DeviceIdType.MESH
BF16 = jnp.bfloat16
F32 = jnp.float32


def slot(dy, dx, dc):
    return (0, 1, 3, 2)[dy] * 4 + dc * 2 + dx


def unslot(s):
    return (0, 1, 3, 2)[s // 4], s % 2, (s // 2) % 2


CHUNKS = (1, 2, 3, 4, 5, 6, 7, 0)
X_FIRST = (2, 6, 7)
STEPS = (
    (0, 0), (1, 0), (2, 0), (3, 0), (0, 1), (4, 0), (1, 1), (2, 1), (5, 0),
    (3, 1), (6, 0), (4, 1), (7, 0), (0, 2), (5, 1), (6, 1), (2, 2), (7, 1),
    (3, 2), (4, 2), (1, 2), (0, 3), (2, 3), (5, 2), (7, 2), (3, 3), (6, 2),
    (4, 3), (1, 3), (5, 3), (7, 3), (6, 3), (1, 4), (5, 4), (6, 4),
)


PARTS = 4
ORDER = (
    "0sum", "1sum", "0own", "2sum", "1own", "3sum", "0a", "0d", "0e", "2own", "1a", "1d", "1e",
    "0h", "0g", "3own", "0n0", "0n1", "0n2", "2a", "2d", "2e", "0n3", "0n4", "0n5", "0n6",
    "1h", "1g", "3a", "1n0", "0o", "1n1", "1n2", "1n3", "1n4", "1n5", "1n6", "0r0", "3d",
    "3e", "0r1", "0r2", "0r3", "0r4", "0r5", "2h", "2g", "0r6", "2n0", "1o", "2n1", "2n2",
    "2n3", "2n4", "2n5", "2n6", "3h", "3g", "1r0", "1r1", "1r2", "1r3", "1r4", "2o", "1r5",
    "1r6", "3n0", "3n1", "3n2", "3n3", "2r0", "2r1", "2r2", "3o", "2r3", "2r4", "2r5", "2r6",
    "3n4", "3n5", "3n6", "3r0", "3r1", "3r2", "3r3", "3r4", "3r5", "3r6",
)


class Links:
    def __init__(self, send_sems, recv_sems):
        t = lax.axis_index("tp")
        self.t = t
        self.g = lax.axis_index("grp")
        self.up = lax.rem(t + 4, 16)
        self.down = lax.rem(t + 12, 16)
        self.over = t + 2 - 4 * lax.rem(lax.div(t, 2), 2)
        self.twin = t + 1 - 2 * lax.rem(t, 2)
        self.send_sems, self.recv_sems = send_sems, recv_sems
        self.started = []
        self.sent = []

    def greet(self):
        barrier = pltpu.get_barrier_semaphore()
        for to in (self.up, self.down, self.over, self.twin):
            pl.semaphore_signal(
                barrier, inc=1, device_id={"tp": to, "grp": self.g}, device_id_type=MESH
            )
        for i in range(1, 8):
            for to in (self.t, self.over):
                pl.semaphore_signal(
                    barrier,
                    inc=1,
                    device_id={"tp": to, "grp": lax.rem(self.g + i, 8)},
                    device_id_type=MESH,
                )

    def greeted(self):
        pl.semaphore_wait(pltpu.get_barrier_semaphore(), 18)

    def send(self, src, dst, tp=None, grp=None):
        n = len(self.started)
        copy = pltpu.make_async_remote_copy(
            src_ref=src,
            dst_ref=dst,
            send_sem=self.send_sems.at[n],
            recv_sem=self.recv_sems.at[n],
            device_id={
                "tp": self.t if tp is None else tp,
                "grp": self.g if grp is None else grp,
            },
            device_id_type=MESH,
        )
        copy.start()
        self.started.append(copy)
        return copy

    def drain(self):
        for copy in self.started:
            if all(copy is not other for other in self.sent):
                copy.wait_send()


def gather_steps(links, piece, whole):
    up, down, over, twin = links.up, links.down, links.over, links.twin
    own, west = slot(0, 0, 0), slot(0, 1, 0)
    below, above, far = slot(3, 0, 0), slot(1, 0, 0), slot(2, 0, 0)
    w_below, w_above, w_far = slot(3, 1, 0), slot(1, 1, 0), slot(2, 1, 0)
    shared, moved = {}, {}

    def share(s):
        shared[s] = [links.send(ref, to, tp=twin) for ref, to in zip(whole(s), whole(s + 2))]

    def here(*slots):
        for s in slots:
            for copy in shared[s]:
                copy.wait_recv()

    def move(name, s, d, h, to):
        moved[name] = links.send(piece(s, h), piece(d, h), tp=to)

    def wait(*names):
        for name in names:
            moved[name].wait_recv()

    def step_own():
        move("a", own, west, 0, over)
        move("d", own, below, 1, up)
        move("e", own, above, 1, down)
        move("b", own, below, 0, up)
        move("c", own, above, 0, down)
        move("f", own, west, 1, over)

    def step_e():
        wait("e")
        move("m", above, far, 1, down)
        move("n", above, w_above, 1, over)

    def step_d():
        wait("d")
        move("l", below, w_below, 1, over)

    def step_a():
        wait("a")
        move("g", west, w_below, 0, up)
        move("h", west, w_above, 0, down)

    def step_f():
        wait("f")
        share(own)

    def step_b():
        wait("b")
        move("i", below, far, 0, up)

    def step_m():
        wait("m")
        move("q", far, w_far, 1, over)

    def step_h():
        wait("c", "n", "h")
        share(above)

    def step_g():
        wait("g")
        move("o", w_below, w_far, 0, up)

    def step_l():
        wait("l")
        share(below)

    def step_o():
        wait("i", "o", "q")
        share(far)

    steps = dict(
        own=step_own, e=step_e, d=step_d, a=step_a, f=step_f, b=step_b,
        m=step_m, h=step_h, g=step_g, l=step_l, o=step_o,
    )
    return steps, functools.partial(here, own, above), functools.partial(here, below, far)


def gather_x_first(links, whole, part, pair):
    up, down, over, twin = links.up, links.down, links.over, links.twin
    own, west = slot(0, 0, 0), slot(0, 1, 0)
    below, above, far = slot(3, 0, 0), slot(1, 0, 0), slot(2, 0, 0)
    w_below, w_above, w_far = slot(3, 1, 0), slot(1, 1, 0), slot(2, 1, 0)
    shared, moved = {}, {}

    def share(s):
        shared[s] = links.send(pair(s), pair(s + 2), tp=twin)

    def here(*slots):
        for s in slots:
            shared[s].wait_recv()

    def move(name, src, dst, to):
        moved[name] = links.send(src, dst, tp=to)

    def wait(*names):
        for name in names:
            moved[name].wait_recv()

    def step_own():
        move("a", whole(own), whole(west), over)
        move("d", whole(own), whole(below), up)
        move("e", whole(own), whole(above), down)

    def step_a():
        wait("a")
        move("g", whole(west), whole(w_below), up)
        move("h", whole(west), whole(w_above), down)
        share(own)

    def step_d():
        wait("d")
        move("k", part(below, 0), part(far, 0), up)

    def step_e():
        wait("e")
        move("m", part(above, 1), part(far, 1), down)

    def step_h():
        wait("h")
        move("p", part(w_above, 1), part(w_far, 1), down)
        share(above)

    def step_g():
        wait("g")
        move("o", part(w_below, 0), part(w_far, 0), up)
        share(below)

    def step_o():
        wait("k", "m", "o", "p")
        share(far)

    steps = dict(own=step_own, a=step_a, d=step_d, e=step_e, h=step_h, g=step_g, o=step_o)
    return steps, functools.partial(here, own, above), functools.partial(here, below, far)


def mix(
    links, q_ref, tok_ref, id_ref, domain_ref,
    k_all, v_all, proj, bias, place, unplace, tops, weight_sums, outs, att, part_out, part_in, disp, x_all, fetch, mixed_ref,
):
    n_rows, width = q_ref.shape
    cap = disp.shape[1] // 8

    def piece(s, h):
        return (k_all, v_all)[h].at[pl.ds(s * n_rows, n_rows)]

    def whole(s):
        return tuple(ref.at[pl.ds(s * n_rows, 2 * n_rows)] for ref in (k_all, v_all))

    t = links.t
    y, x, core = lax.div(t, 4), lax.rem(lax.div(t, 2), 2), lax.rem(t, 2)

    def set_bias():
        for s in range(16):
            dy, dx, dc = unslot(s)
            if s == 0:
                row = lax.broadcasted_iota(jnp.int32, (n_rows, n_rows), 0)
                col = lax.broadcasted_iota(jnp.int32, (n_rows, n_rows), 1)
                bias[:, 0:n_rows] = jnp.where(col <= row, 0.0, NEG_FILL)
            else:
                from_y = lax.rem(y + dy, 4)
                from_x = x + dx - 2 * x * dx
                from_core = core + dc - 2 * core * dc
                hidden = (from_y * 4 + from_x * 2 + from_core > t).astype(F32)
                bias[:, s * n_rows : (s + 1) * n_rows] = (
                    jnp.full((n_rows, n_rows), NEG_FILL, F32) * hidden
                )

    def set_place():
        eye = lax.broadcasted_iota(jnp.int32, (8, 8), 0) == lax.broadcasted_iota(
            jnp.int32, (8, 8), 1
        )
        domains = jnp.sum(jnp.where(eye, domain_ref[...], 0), axis=1, keepdims=True)
        hit = (domains == id_ref[...]).astype(F32)
        upto = lax.broadcasted_iota(jnp.int32, (n_rows, n_rows), 0) <= lax.broadcasted_iota(
            jnp.int32, (n_rows, n_rows), 1
        )
        count = jnp.dot(hit.astype(BF16), upto.astype(BF16), preferred_element_type=F32) * hit
        nth = lax.broadcasted_iota(jnp.int32, (cap, n_rows), 0).astype(F32) + 1.0
        parts = [(count[e : e + 1] == nth).astype(F32) for e in range(8)]
        placed = jnp.concatenate(parts, 0)
        place[...] = placed.astype(BF16)
        unplace[...] = placed.T.astype(BF16)

    lane = lax.broadcasted_iota(jnp.int32, (n_rows, LANES), 1)
    low = lane < HD
    log2_scale = math.log2(math.e) / math.sqrt(HD)

    n_near = 8 * n_rows

    def attend(p, first):
        cols = pl.ds(pl.multiple_of(p * LANES, LANES), LANES)
        keys = pl.ds(0 if first else n_near, n_near)
        q_pair = q_ref[:, cols]
        zero = jnp.zeros_like(q_pair)
        q_two = jnp.concatenate([jnp.where(low, q_pair, zero), jnp.where(low, zero, q_pair)], 0)
        s = lax.dot_general(
            q_two, k_all[keys, cols], (((1,), (1,)), ((), ())), preferred_element_type=F32
        )
        hide = bias[:, 0:n_near] if first else bias[:, n_near:]
        s = s + jnp.concatenate([hide, hide], 0)
        top = jnp.max(s, axis=1, keepdims=True)
        if not first:
            top = jnp.maximum(top, tops[p])
        w = jnp.exp2((s - top) * log2_scale)
        total = jnp.sum(w, axis=1, keepdims=True)
        o = jnp.dot(w.astype(BF16), v_all[keys, cols], preferred_element_type=F32)
        if first:
            tops[p], weight_sums[p], outs[p] = top, total, o
        else:
            shrink = jnp.exp2((tops[p] - top) * log2_scale)
            o = (o + outs[p] * shrink) / (total + weight_sums[p] * shrink)
            att[:, cols] = jnp.where(low, o[0:n_rows], o[n_rows:]).astype(BF16)

    def attend_all(first):
        @pl.loop(0, width // LANES)
        def _(p):
            attend(p, first)

    steps, near, rest = gather_steps(links, piece, whole)
    steps["own"]()
    set_place()
    set_bias()
    for name in ("e", "d", "a", "f", "b", "m", "h", "g"):
        steps[name]()
    near()
    attend_all(True)
    for name in ("l", "o"):
        steps[name]()
    rest()
    attend_all(False)

    fetch.wait()
    part_width = width // PARTS
    others = (1, 2, 3, 4, 5, 6, 7)
    totals = []
    sums = [dict() for _ in range(PARTS)]

    def project(i, c):
        at = lax.rem(links.g + i, 8) * width + c * part_width
        cols = pl.ds(pl.multiple_of(at, part_width), part_width)
        return jnp.dot(att[...], proj[:, cols], preferred_element_type=F32)

    def send_part(i, c):
        sums[c][i] = links.send(part_out.at[c, i], part_in.at[c, i], grp=lax.rem(links.g + i, 8))

    for c in range(PARTS):
        for i in others:
            part_out[c, i] = project(i, c).astype(BF16)
            if c == 0:
                send_part(i, c)
        tokens = tok_ref[:, c * part_width : (c + 1) * part_width]
        totals.append(project(0, c) + tokens.astype(F32))
    for i in others:
        sums[0][i].wait_send()
        links.sent.append(sums[0][i])
        send_part(i, 1)

    mine = pl.ds(pl.multiple_of(links.g * part_width, part_width), part_width)
    moved = [dict() for _ in range(PARTS)]

    def sum_up(c):
        total = totals[c]
        for i in others:
            sums[c][i].wait_recv()
            if c + 2 < PARTS:
                send_part(i, c + 2)
            total = total + part_in[c, i].astype(F32)
        mixed = total.astype(BF16)
        mixed_ref[:, c * part_width : (c + 1) * part_width] = mixed
        disp[c] = jnp.dot(place[...], mixed, preferred_element_type=F32).astype(BF16)
        for i in others:
            to = lax.rem(links.g + i, 8)
            chosen = disp.at[c, pl.ds(pl.multiple_of(to * cap, cap), cap)]
            moved[c][i] = links.send(chosen, x_all.at[c, pl.ds(0, cap), mine], grp=to)
        x_all[c, 0:cap, mine] = disp[c, pl.ds(pl.multiple_of(links.g * cap, cap), cap)]

    def rows_here(c):
        for i in others:
            moved[c][i].wait_recv()

    return sum_up, rows_here


def experts(
    links, x_all, gate_up, down, act,
    own_sum, core_out, core_in, y_out, y_in, n_out, n_in, x_out, x_in, fin_out, fin_a, fin_b,
    loads, load_down, sum_up, rows_here,
):
    cap, width = x_all.shape[1] // 16, PARTS * x_all.shape[2]
    part_width = width // PARTS
    tiles = act.shape[1] // LANES
    half_rows = 8 * cap
    chunk = width // 8
    half_chunk = chunk // 2

    def blocks(c):
        def part(s, h):
            return x_all.at[c, pl.ds(s * cap, cap), pl.ds(h * (part_width // 2), part_width // 2)]

        return (
            lambda s: x_all.at[c, pl.ds(s * cap, cap)],
            part,
            lambda s: x_all.at[c, pl.ds(s * cap, 2 * cap)],
        )

    gathers = [gather_x_first(links, *blocks(c)) for c in range(PARTS)]
    tile = 2 * LANES

    def product(c, m, j):
        w = gate_up[c, :, :, j * tile : (j + 1) * tile].reshape(part_width, tile)
        rows = x_all[c, m * half_rows : (m + 1) * half_rows, :]
        return jnp.dot(rows, w, preferred_element_type=F32)

    def work(c, m, j):
        at = slice(m * tile, (m + 1) * tile)
        both = product(c, m, j)
        if c > 0:
            both = own_sum[j, :, at] + both
        if c < PARTS - 1:
            own_sum[j, :, at] = both
            return
        gate, lift = both[:, :LANES], both[:, LANES:]
        act[m * half_rows : (m + 1) * half_rows, j * LANES : (j + 1) * LANES] = (
            gate / (1.0 + jnp.exp(-gate)) * lift
        ).astype(BF16)

    for name in ORDER:
        c, at = int(name[0]), name[1:]
        if at == "sum":
            sum_up(c)
        elif at[0] in "nr":
            m = "nr".index(at[0])
            if at[1] == "0":
                gathers[c][1 + m]()
                if name == "0n0":
                    for load in loads:
                        load.wait()
            work(c, m, int(at[1]))
        else:
            if at == "own":
                rows_here(c)
            gathers[c][0][at]()
    load_down.wait()

    copies = [dict() for _ in range(8)]
    pair = 2 * cap
    near_up, near_down, far = (1, 2, 3)
    x_at = {i: n for n, i in enumerate(X_FIRST)}

    def start(i):
        to = lax.rem(links.g + i, 8)
        cols = pl.ds(pl.multiple_of(to * chunk, chunk), chunk)
        out = jnp.dot(act[...], down[:, cols], preferred_element_type=F32)
        for b in range(4):
            core_out[i, b * pair : (b + 1) * pair] = out[
                (2 * b + 1) * pair : (2 * b + 2) * pair
            ].astype(BF16)
        copies[i]["core"] = links.send(core_out.at[i], core_in.at[i], tp=links.twin)
        for b in range(4):
            own_sum[i, b * pair : (b + 1) * pair] = out[2 * b * pair : (2 * b + 1) * pair]

    def core_sum(i):
        copies[i]["core"].wait_recv()
        own_sum[i] = own_sum[i] + core_in[i].astype(F32)

    def y_far(i, n):
        rows = pl.ds(far * n, n)
        y_out[i, 0, 0:n] = own_sum[i, rows, 0:half_chunk].astype(BF16)
        y_out[i, 1, 0:n] = own_sum[i, rows, half_chunk:].astype(BF16)
        for s, to in ((0, links.up), (1, links.down)):
            copies[i]["far", s] = links.send(
                y_out.at[i, s, pl.ds(0, n)], y_in.at[i, s, pl.ds(0, n)], tp=to
            )

    def y_near(i, n):
        for s, at, to in ((0, near_up, links.up), (1, near_down, links.down)):
            copies[i]["far", s].wait_recv()
            block = own_sum[i, at * n : (at + 1) * n]
            left, right = block[:, 0:half_chunk], block[:, half_chunk:]
            passing = y_in[i, s, 0:n].astype(F32)
            left, right = (left + passing, right) if s == 0 else (left, right + passing)
            n_out[i, s, 0:n, 0:half_chunk] = left.astype(BF16)
            n_out[i, s, 0:n, half_chunk:] = right.astype(BF16)
            copies[i]["near", s] = links.send(
                n_out.at[i, s, pl.ds(0, n)], n_in.at[i, s, pl.ds(0, n)], tp=to
            )

    def y_sum(i, n):
        for s in range(2):
            copies[i]["near", s].wait_recv()
        return own_sum[i, 0:n] + n_in[i, 0, 0:n].astype(F32) + n_in[i, 1, 0:n].astype(F32)

    mine = pl.ds(pl.multiple_of(links.g * cap, cap), cap)

    def finish(i, total, side, into, tp):
        if i == 0 and tp is links.t:
            into[mine, :] = total.astype(BF16)
        else:
            at = pl.ds(side * cap, cap)
            fin_out[i, at] = total.astype(BF16)
            copies[i]["fin", side] = links.send(
                fin_out.at[i, at], into.at[mine], tp=tp, grp=lax.rem(links.g + i, 8)
            )

    def stage(i, step):
        if step == 0:
            start(i)
        elif i not in x_at:
            if step == 1:
                core_sum(i)
                y_far(i, pair)
            elif step == 2:
                y_near(i, pair)
            else:
                total = y_sum(i, pair)
                finish(i, total[cap:], 1, fin_b, links.over)
                finish(i, total[0:cap], 0, fin_a, links.t)
        elif step == 1:
            core_sum(i)
            for b in range(4):
                x_out[x_at[i], b * cap : (b + 1) * cap] = own_sum[
                    i, (2 * b + 1) * cap : (2 * b + 2) * cap
                ].astype(BF16)
            copies[i]["x"] = links.send(x_out.at[x_at[i]], x_in.at[x_at[i]], tp=links.over)
        elif step == 2:
            copies[i]["x"].wait_recv()
            for b in range(4):
                own_sum[i, b * cap : (b + 1) * cap] = own_sum[
                    i, 2 * b * cap : (2 * b + 1) * cap
                ] + x_in[x_at[i], b * cap : (b + 1) * cap].astype(F32)
            y_far(i, cap)
        elif step == 3:
            y_near(i, cap)
        else:
            finish(i, y_sum(i, cap), 0, fin_a, links.t)

    for i in X_FIRST:
        rows = pl.ds(pl.multiple_of(lax.rem(links.g + 8 - i, 8) * cap, cap), cap)
        fin_b[rows, :] = jnp.zeros((cap, chunk), BF16)
    for at, step in STEPS:
        stage(CHUNKS[at], step)
    for i in range(8):
        for side in range(2):
            if ("fin", side) in copies[i]:
                copies[i]["fin", side].wait_recv()


def layer_kernel(
    q_ref, k_ref, v_ref, tok_ref, id_ref, domain_ref, proj_ref, gate_ref, up_ref, down_ref,
    out_ref,
    q_own, tok_own, mixed_ref, k_all, v_all, proj, bias, place, unplace, tops, weight_sums, outs, att, part_out, part_in, disp,
    x_all, gate_up, down, act,
    own_sum, core_out, core_in, y_out, y_in, n_out, n_in, x_out, x_in, fin_out, fin_a, fin_b,
    send_sems, recv_sems, load_sems,
):
    links = Links(send_sems, recv_sems)
    n_rows = q_ref.shape[0]
    tiles = act.shape[1] // LANES
    fetch = pltpu.make_async_copy(proj_ref, proj, load_sems.at[1])
    load_down = pltpu.make_async_copy(down_ref.at[0], down, load_sems.at[0])
    loads = []
    for c in range(PARTS):
        for j in range(tiles):
            for ref, at in ((gate_ref, 2 * j), (up_ref, 2 * j + 1)):
                loads.append(
                    pltpu.make_async_copy(
                        ref.at[:, c, :, pl.ds(j * LANES, LANES)],
                        gate_up.at[c, :, :, pl.ds(at * LANES, LANES)],
                        load_sems.at[6 + c * 2 * tiles + at],
                    )
                )
    own_rows = pl.ds(0, n_rows)
    first = [
        pltpu.make_async_copy(ref, to, load_sems.at[2 + n])
        for n, (ref, to) in enumerate(
            (
                (k_ref, k_all.at[own_rows]),
                (v_ref, v_all.at[own_rows]),
                (q_ref, q_own),
                (tok_ref, tok_own),
            )
        )
    ]
    links.greet()
    for load in first:
        load.start()
    for load in first:
        load.wait()
    links.greeted()
    for load in (fetch, *loads, load_down):
        load.start()
    sum_up, rows_here = mix(
        links, q_own, tok_own, id_ref, domain_ref,
        k_all, v_all, proj, bias, place, unplace, tops, weight_sums, outs, att,
        part_out, part_in, disp, x_all, fetch, mixed_ref,
    )
    experts(
        links, x_all, gate_up, down, act,
        own_sum, core_out, core_in, y_out, y_in, n_out, n_in, x_out, x_in, fin_out, fin_a, fin_b,
        loads, load_down, sum_up, rows_here,
    )
    fin = (fin_a[...].astype(F32) + fin_b[...].astype(F32)).astype(BF16)
    ffn = jnp.dot(unplace[...], fin, preferred_element_type=F32)
    out_ref[...] = (mixed_ref[...].astype(F32) + ffn).astype(BF16)
    links.drain()


def shards(
    tokens_in,
    queries,
    keys_all,
    values_all,
    out_proj,
    domain_ids,
    expert_domain,
    gate_proj,
    up_proj,
    down_proj,
):
    n_rows, width = queries.shape
    model = out_proj.shape[1]
    hidden = gate_proj.shape[2]
    cap = n_rows // 4
    chunk = model // 8
    vmem = pl.BlockSpec(memory_space=pltpu.VMEM)
    hbm = pl.BlockSpec(memory_space=pl.ANY)

    return pl.pallas_call(
        layer_kernel,
        out_shape=jax.ShapeDtypeStruct((n_rows, width), BF16),
        in_specs=[hbm] * 4 + [vmem] * 2 + [hbm] * 4,
        out_specs=vmem,
        scratch_shapes=[
            pltpu.VMEM((n_rows, width), BF16),
            pltpu.VMEM((n_rows, width), BF16),
            pltpu.VMEM((n_rows, width), BF16),
            pltpu.VMEM((16 * n_rows, width), BF16),
            pltpu.VMEM((16 * n_rows, width), BF16),
            pltpu.VMEM((width, model), BF16),
            pltpu.VMEM((n_rows, 16 * n_rows), F32),
            pltpu.VMEM((8 * cap, n_rows), BF16),
            pltpu.VMEM((n_rows, 8 * cap), BF16),
            pltpu.VMEM((width // LANES, 2 * n_rows, 1), F32),
            pltpu.VMEM((width // LANES, 2 * n_rows, 1), F32),
            pltpu.VMEM((width // LANES, 2 * n_rows, LANES), F32),
            pltpu.VMEM((n_rows, width), BF16),
            pltpu.VMEM((PARTS, 8, n_rows, width // PARTS), BF16),
            pltpu.VMEM((PARTS, 8, n_rows, width // PARTS), BF16),
            pltpu.VMEM((PARTS, 8 * cap, width // PARTS), BF16),
            pltpu.VMEM((PARTS, 16 * cap, model // PARTS), BF16),
            pltpu.VMEM((PARTS, 8, chunk // PARTS, 2 * hidden), BF16),
            pltpu.VMEM((hidden, model), BF16),
            pltpu.VMEM((16 * cap, hidden), BF16),
            pltpu.VMEM((8, 8 * cap, chunk), F32),
            pltpu.VMEM((8, 8 * cap, chunk), BF16),
            pltpu.VMEM((8, 8 * cap, chunk), BF16),
            pltpu.VMEM((8, 2, 2 * cap, chunk // 2), BF16),
            pltpu.VMEM((8, 2, 2 * cap, chunk // 2), BF16),
            pltpu.VMEM((8, 2, 2 * cap, chunk), BF16),
            pltpu.VMEM((8, 2, 2 * cap, chunk), BF16),
            pltpu.VMEM((len(X_FIRST), 4 * cap, chunk), BF16),
            pltpu.VMEM((len(X_FIRST), 4 * cap, chunk), BF16),
            pltpu.VMEM((8, 2 * cap, chunk), BF16),
            pltpu.VMEM((8 * cap, chunk), BF16),
            pltpu.VMEM((8 * cap, chunk), BF16),
            pltpu.SemaphoreType.DMA((272,)),
            pltpu.SemaphoreType.DMA((272,)),
            pltpu.SemaphoreType.DMA((2 * PARTS * (hidden // LANES) + 6,)),
        ],
        compiler_params=pltpu.CompilerParams(
            collective_id=0, has_side_effects=True, vmem_limit_bytes=62 * 2**20
        ),
        name="layer",
    )(
        queries, keys_all, values_all, tokens_in,
        domain_ids.reshape(1, n_rows), expert_domain.reshape(1, 8),
        out_proj,
        gate_proj.reshape(8, PARTS, chunk // PARTS, hidden),
        up_proj.reshape(8, PARTS, chunk // PARTS, hidden),
        down_proj,
    )


def solution(mesh):
    in_specs = (
        P("tp", "grp"),
        P("tp", "grp"),
        P("tp", "grp"),
        P("tp", "grp"),
        P("grp", None),
        P("tp", None),
        P(),
        P("grp", None, "tp"),
        P("grp", None, "tp"),
        P("grp", "tp", None),
    )
    out_specs = P("tp", "grp")
    return jax.shard_map(shards, mesh=mesh, in_specs=in_specs, out_specs=out_specs, check_vma=False)
```

time: 108 us -> 102 us (0.944)
  Pallas kernels: 104 us -> 99.9 us
  other arithmetic: 2.72 us -> 0 us
    pallas_call x1, Pallas kernels: 104 us -> 99.9 us  [shards(): pl.pallas_call(layer_kernel, out_shape=jax.ShapeDtypeStruct((n_rows, widt...]
    convert_element_type x3 -> x0, other arithmetic: 2.44 us -> none  [the longest x1 1.67 us: shards(): return (mixed.astype(F32) + ffn).astype(BF16)]
    unnamed x2 -> x1, local copies, waits for them, and re-layouts: 0.01 us -> 1.57 us
where the time goes in v3:
time: 102 us; the launch traced here: 101 us
  Pallas kernels  99.9 us (98%)
  local copies, waits for them, and re-layouts  1.57 us (2%)
    pallas_call x1, Pallas kernels, shards(): pl.pallas_call(layer_kernel, out_shape=jax.ShapeDtypeStruct((n_rows, widt...  99.9 us

profile of v3, /device:TPU:0, one launch (start us, length us, event | category | flops | bytes accessed | tf_op | source)
XLA Modules:
  0.0 101.4 jit_solution(13528221019126545575)
XLA Ops:
  0.0 99.9 %layer.1 = bf16[128,512]{1,0:T(8,128)(2,1)} custom-call(bf16[128,512]{1,0:T(8,128)(2,1)} %q_ref.1, bf16[128,512]{1,0:T(8,128)(2,1)} %k_ref.1, bf16[128,512]{1,0:T(8,128)(2,1)} %v_ref.1, bf16[128,512]{1,0:T(8,128)(2,1)} %tok_ref.1, s32[1,128]{1,0:T(1,128)} %bitcast.6, s32[1,8]{1,0:T(1,128)} %bitcast.7, bf16[512,4096]{1,0:T(8,128)(2,1)} %proj_ref.1, ...), custom_call_target="tpu_custom_call" | custom-call | tf_op jit(solution)/shard_map/layer/pallas_call | solution.py:632
  99.9 1.6 %copy.12 = bf16[128,512]{1,0:T(8,128)(2,1)} copy(bf16[128,512]{1,0:T(8,128)(2,1)} %layer.1) | data formatting | bytes 262144

commit v4 on v3

--- a/solution.py
+++ b/solution.py
@@ -300,8 +300,11 @@
         s = lax.dot_general(
             q_two, k_all[keys, cols], (((1,), (1,)), ((), ())), preferred_element_type=F32
         )
-        hide = bias[:, 0:n_near] if first else bias[:, n_near:]
-        s = s + jnp.concatenate([hide, hide], 0)
+        if first:
+            hide = bias[:, 0:n_near]
+            s = s + jnp.concatenate([hide, hide], 0)
+        else:
+            s = s + bias[0:1, n_near:]
         top = jnp.max(s, axis=1, keepdims=True)
         if not first:
             top = jnp.maximum(top, tops[p])

time: 102 us -> 102 us (level)
  no operation moved by 1% of the time
where the time goes in v4:
time: 102 us; the launch traced here: 101 us
  Pallas kernels  99.9 us (98%)
  local copies, waits for them, and re-layouts  1.57 us (2%)
    pallas_call x1, Pallas kernels, shards(): pl.pallas_call(layer_kernel, out_shape=jax.ShapeDtypeStruct((n_rows, widt...  99.9 us

profile of v4, /device:TPU:0, one launch (start us, length us, event | category | flops | bytes accessed | tf_op | source)
XLA Modules:
  0.0 101.5 jit_solution(15089916375966497989)
XLA Ops:
  0.0 99.9 %layer.1 = bf16[128,512]{1,0:T(8,128)(2,1)} custom-call(bf16[128,512]{1,0:T(8,128)(2,1)} %q_ref.1, bf16[128,512]{1,0:T(8,128)(2,1)} %k_ref.1, bf16[128,512]{1,0:T(8,128)(2,1)} %v_ref.1, bf16[128,512]{1,0:T(8,128)(2,1)} %tok_ref.1, s32[1,128]{1,0:T(1,128)} %bitcast.6, s32[1,8]{1,0:T(1,128)} %bitcast.7, bf16[512,4096]{1,0:T(8,128)(2,1)} %proj_ref.1, ...), custom_call_target="tpu_custom_call" | custom-call | tf_op jit(solution)/shard_map/layer/pallas_call | solution.py:635
  99.9 1.6 %copy.12 = bf16[128,512]{1,0:T(8,128)(2,1)} copy(bf16[128,512]{1,0:T(8,128)(2,1)} %layer.1) | data formatting | bytes 262144
